TPU v7x, 32 devices: a whole 2x2x4 slice. The times are simulated.
32 devices in a mesh: dp: 8 (over z, x), tensor: 4 (over y, core).
Axes of the slice: x: 2, y: 2, z: 4, core: 2. Of those that a mesh axis runs over, the one named last changes fastest.
Arguments:
- hidden_in: bfloat16 [8192, 1152], P(('dp', 'tensor')), may hold values from -6 to 6
- picture_ids: int32 [8192], P('dp'), may hold values from -1 to 9, as said below
- norm1_gain: float32 [1152], replicated, may hold values from 0.5 to 1.5
- norm1_bias: float32 [1152], replicated, may hold values from -1.75 to 1.75
- w_qkv: bfloat16 [3, 1152, 1152], P(None, None, 'tensor'), may hold values from -1 to 1
- qv_bias: float32 [2, 1152], P(None, 'tensor'), may hold values from -3 to 3
- w_out: bfloat16 [1152, 1152], P('tensor'), may hold values from -0.75 to 0.75
- out_bias: float32 [1152], replicated, may hold values from -1.75 to 1.75
- norm2_gain: float32 [1152], replicated, may hold values from 0.5 to 1.5
- norm2_bias: float32 [1152], replicated, may hold values from -1.75 to 1.75
- w_up: bfloat16 [1152, 4304], P(None, 'tensor'), may hold values from -0.1875 to 0.1875
- up_bias: float32 [4304], P('tensor'), may hold values from -3 to 3
- w_down: bfloat16 [4304, 1152], P('tensor'), may hold values from -0.125 to 0.125
- down_bias: float32 [1152], replicated, may hold values from -1.75 to 1.75
- cotangent: bfloat16 [8192, 1152], P(('dp', 'tensor')), may hold values from -6 to 6
Outputs:
- hidden_out: bfloat16 [8192, 1152], P(('dp', 'tensor'))
- grad_in: bfloat16 [8192, 1152], P(('dp', 'tensor'))
- grad_qkv: float32 [3, 1152, 1152], P(None, 'dp', 'tensor')
- grad_out: float32 [1152, 1152], P('tensor', 'dp')
- grad_up: float32 [1152, 4304], P('dp', 'tensor')
- grad_down: float32 [4304, 1152], P('tensor', 'dp')
- grad_qv_bias: float32 [2, 1152], P(None, 'tensor')
- grad_up_bias: float32 [4304], P('tensor')
- grad_shared: float32 [6, 1152], replicated
- head_maxima: float32 [16], P('tensor')
- scaled_qk: bfloat16 [2, 1152, 1152], P(None, None, 'tensor')
- scaled_query_bias: float32 [1152], P('tensor')
Inputs may be any that keep to these rules, and one draw needn't show every extreme that they name: `picture_ids`: each aligned row of 1024 tokens holds whole pictures of 100 to 1024 patches one after another, numbered from 0 within the row, then padding with id -1; some row holds a single picture of 1024 patches, and some other row holds 10 pictures of 100 patches.
All inputs are finite; a program needn't handle non-finite values.
Results may differ from a plain program's by a relative error of at most 0.014.
Values may be sent and summed in bfloat16 or wider, within the bound.
No kernel may reach another device: no remote copies, remote signals or barrier semaphores. Data moves between devices by JAX's collectives and lax.ppermute only.
A program may use at most 192 MiB of HBM per device.

v0:
```python
import jax
import jax.numpy as jnp
from jax import lax
from jax.sharding import PartitionSpec as P

HEAD_DIM = 72
PACK = 1024
QBLOCK = 512
CLIP_LIMIT = 9
eps_norm = 1e-06
neg_fill = -1e30


def normalize(values_in, gain, shift):
    row_mean = jnp.mean(values_in, axis=-1, keepdims=True)
    centred = values_in - row_mean
    variance = jnp.mean(centred * centred, axis=-1, keepdims=True)
    inverse = lax.rsqrt(variance + eps_norm)
    unit_rows = centred * inverse
    return (unit_rows * gain + shift, unit_rows, inverse)


def norm_back(grad_rows, unit_rows, inverse, gain):
    scaled = grad_rows * gain
    return inverse * (
        scaled
        - jnp.mean(scaled, axis=-1, keepdims=True)
        - unit_rows * jnp.mean(scaled * unit_rows, axis=-1, keepdims=True)
    )


def gelu_tanh(inputs):
    return jax.nn.gelu(inputs, approximate=True)


def local(
    hidden_in,
    picture_ids,
    norm1_gain,
    norm1_bias,
    w_qkv,
    qv_bias,
    w_out,
    out_bias,
    norm2_gain,
    norm2_bias,
    w_up,
    up_bias,
    w_down,
    down_bias,
    cotangent,
):
    group_rows = picture_ids.shape[0]
    row_count = group_rows // PACK
    head_width = w_qkv.shape[2]
    local_heads = head_width // HEAD_DIM
    score_scale = HEAD_DIM ** (-0.5)
    block_count = PACK // QBLOCK
    block_shape = (row_count, block_count, QBLOCK, local_heads, HEAD_DIM)
    row_shape = (row_count, PACK, local_heads, HEAD_DIM)
    source = hidden_in.astype(jnp.float32)
    normed_a, unit_a, inverse_a = normalize(source, norm1_gain, norm1_bias)
    whole_a = lax.all_gather(normed_a.astype(jnp.bfloat16), "tensor", axis=0, tiled=True)
    projected = jnp.einsum("td,cde->cte", whole_a, w_qkv, preferred_element_type=jnp.float32)
    queries = (projected[0] + qv_bias[0]).astype(jnp.bfloat16)
    key_rows = projected[1].astype(jnp.bfloat16)
    values = (projected[2] + qv_bias[1]).astype(jnp.bfloat16)
    query_blocks = queries.reshape(block_shape)
    key_heads = key_rows.reshape(row_shape)
    value_heads = values.reshape(row_shape)
    row_ids = picture_ids.reshape(row_count, PACK)

    def attend_row(parts_in):
        row_q, row_k, row_v, ids_row = parts_in
        block_ids = ids_row.reshape(block_count, QBLOCK)

        def attend_block(block_in):
            block_q, query_ids = block_in
            scores = (
                jnp.einsum("qhd,khd->hqk", block_q, row_k, preferred_element_type=jnp.float32)
                * score_scale
            )
            allowed = query_ids[:, None] == ids_row[None, :]
            scores = jnp.where(allowed[None], scores, neg_fill)
            row_top = jnp.max(scores, axis=2, keepdims=True)
            weights = jnp.exp(scores - row_top)
            row_sum = jnp.sum(weights, axis=2, keepdims=True)
            prob_rows = (weights / row_sum).astype(jnp.bfloat16)
            attended = jnp.einsum(
                "hqk,khd->qhd", prob_rows, row_v, preferred_element_type=jnp.float32
            )
            return (
                attended.astype(jnp.bfloat16),
                (row_top + jnp.log(row_sum))[:, :, 0],
                jnp.max(row_top[:, :, 0], axis=1),
            )

        return lax.map(attend_block, (row_q, block_ids))

    attended, log_total, block_top = lax.map(
        attend_row, (query_blocks, key_heads, value_heads, row_ids)
    )
    flat_att = attended.reshape(group_rows, head_width)
    branch_a = lax.psum_scatter(
        jnp.dot(flat_att, w_out, preferred_element_type=jnp.float32),
        "tensor",
        scatter_dimension=0,
        tiled=True,
    )
    residual = source + branch_a + out_bias
    normed_b, unit_b, inverse_b = normalize(residual, norm2_gain, norm2_bias)
    whole_b = lax.all_gather(normed_b.astype(jnp.bfloat16), "tensor", axis=0, tiled=True)
    pre_act = jnp.dot(whole_b, w_up, preferred_element_type=jnp.float32) + up_bias
    activated = gelu_tanh(pre_act).astype(jnp.bfloat16)
    branch_b = lax.psum_scatter(
        jnp.dot(activated, w_down, preferred_element_type=jnp.float32).astype(jnp.bfloat16),
        "tensor",
        scatter_dimension=0,
        tiled=True,
    ).astype(jnp.float32)
    hidden_out = (residual + branch_b + down_bias).astype(jnp.bfloat16)
    head_maxima = lax.pmax(jnp.max(block_top, axis=(0, 1)), "dp")
    limit = jnp.float32(CLIP_LIMIT)
    factor = jnp.sqrt(limit / jnp.maximum(head_maxima, limit))
    column = jnp.repeat(factor, HEAD_DIM)
    scaled_qk = (w_qkv[:2].astype(jnp.float32) * column).astype(jnp.bfloat16)
    scaled_query_bias = qv_bias[0] * column
    whole_grad = lax.all_gather(cotangent, "tensor", axis=0, tiled=True)
    grad_act = jnp.einsum("td,fd->tf", whole_grad, w_down, preferred_element_type=jnp.float32)
    grad_pre = jax.vjp(gelu_tanh, pre_act)[1](grad_act)[0].astype(jnp.bfloat16)
    grad_down = jnp.einsum("tf,td->fd", activated, whole_grad, preferred_element_type=jnp.float32)
    grad_up = jnp.einsum("td,tf->df", whole_b, grad_pre, preferred_element_type=jnp.float32)
    grad_up_bias = jnp.sum(grad_pre, axis=0, dtype=jnp.float32)
    grad_norm_b = lax.psum_scatter(
        jnp.einsum("tf,df->td", grad_pre, w_up, preferred_element_type=jnp.float32),
        "tensor",
        scatter_dimension=0,
        tiled=True,
    )
    grad_top = cotangent.astype(jnp.float32)
    grad_resid = grad_top + norm_back(grad_norm_b, unit_b, inverse_b, norm2_gain)
    grad_branch = grad_resid.astype(jnp.bfloat16)
    whole_branch = lax.all_gather(grad_branch, "tensor", axis=0, tiled=True)
    grad_out = jnp.einsum("te,td->ed", flat_att, whole_branch, preferred_element_type=jnp.float32)
    grad_att = jnp.einsum(
        "td,ed->te", whole_branch, w_out, preferred_element_type=jnp.float32
    ).astype(jnp.bfloat16)

    def back_row(parts_in):
        row_q, row_k, row_v, ids_row, row_grad, row_lse = parts_in
        block_ids = ids_row.reshape(block_count, QBLOCK)

        def back_block(state_in, block_in):
            key_grad, value_grad = state_in
            block_q, query_ids, block_grad, block_lse = block_in
            scores = (
                jnp.einsum("qhd,khd->hqk", block_q, row_k, preferred_element_type=jnp.float32)
                * score_scale
            )
            allowed = query_ids[:, None] == ids_row[None, :]
            scores = jnp.where(allowed[None], scores, neg_fill)
            prob_full = jnp.exp(scores - block_lse[:, :, None])
            grad_probs = jnp.einsum(
                "qhd,khd->hqk", block_grad, row_v, preferred_element_type=jnp.float32
            )
            inner = jnp.sum(prob_full * grad_probs, axis=2, keepdims=True)
            grad_scores = (prob_full * (grad_probs - inner)).astype(jnp.bfloat16)
            query_grad = (
                jnp.einsum("hqk,khd->qhd", grad_scores, row_k, preferred_element_type=jnp.float32)
                * score_scale
            )
            key_grad = (
                key_grad
                + jnp.einsum(
                    "hqk,qhd->khd", grad_scores, block_q, preferred_element_type=jnp.float32
                )
                * score_scale
            )
            value_grad = value_grad + jnp.einsum(
                "hqk,qhd->khd",
                prob_full.astype(jnp.bfloat16),
                block_grad,
                preferred_element_type=jnp.float32,
            )
            return ((key_grad, value_grad), query_grad.astype(jnp.bfloat16))

        zero_rows = jnp.zeros(row_k.shape, jnp.float32)
        (key_grad, value_grad), query_grad = lax.scan(
            back_block, (zero_rows, zero_rows), (row_q, block_ids, row_grad, row_lse)
        )
        return (query_grad, key_grad.astype(jnp.bfloat16), value_grad.astype(jnp.bfloat16))

    query_grad, key_grad, value_grad = lax.map(
        back_row,
        (query_blocks, key_heads, value_heads, row_ids, grad_att.reshape(block_shape), log_total),
    )
    grad_stack = jnp.stack(
        [
            query_grad.reshape(group_rows, head_width),
            key_grad.reshape(group_rows, head_width),
            value_grad.reshape(group_rows, head_width),
        ]
    )
    grad_qkv = jnp.einsum("td,cte->cde", whole_a, grad_stack, preferred_element_type=jnp.float32)
    grad_qv_bias = jnp.stack(
        [
            jnp.sum(grad_stack[0], axis=0, dtype=jnp.float32),
            jnp.sum(grad_stack[2], axis=0, dtype=jnp.float32),
        ]
    )
    grad_norm_a = lax.psum_scatter(
        jnp.einsum("cte,cde->td", grad_stack, w_qkv, preferred_element_type=jnp.float32),
        "tensor",
        scatter_dimension=0,
        tiled=True,
    )
    grad_in = (grad_resid + norm_back(grad_norm_a, unit_a, inverse_a, norm1_gain)).astype(
        jnp.bfloat16
    )
    grad_qkv, grad_out, grad_up, grad_down = (
        lax.psum_scatter(grad_qkv, "dp", scatter_dimension=1, tiled=True),
        lax.psum_scatter(grad_out, "dp", scatter_dimension=1, tiled=True),
        lax.psum_scatter(grad_up, "dp", scatter_dimension=0, tiled=True),
        lax.psum_scatter(grad_down, "dp", scatter_dimension=1, tiled=True),
    )
    grad_qv_bias, grad_up_bias = lax.psum((grad_qv_bias, grad_up_bias), "dp")
    shared_part = jnp.stack(
        [
            jnp.sum(grad_norm_a * unit_a, axis=0),
            jnp.sum(grad_norm_a, axis=0),
            jnp.sum(grad_resid, axis=0),
            jnp.sum(grad_norm_b * unit_b, axis=0),
            jnp.sum(grad_norm_b, axis=0),
            jnp.sum(grad_top, axis=0),
        ]
    )
    grad_shared = lax.psum(shared_part, ("dp", "tensor"))
    return (
        hidden_out,
        grad_in,
        grad_qkv,
        grad_out,
        grad_up,
        grad_down,
        grad_qv_bias,
        grad_up_bias,
        grad_shared,
        head_maxima,
        scaled_qk,
        scaled_query_bias,
    )


def solution(mesh):
    return jax.shard_map(
        local,
        mesh=mesh,
        in_specs=(
            P(("dp", "tensor"), None),
            P("dp"),
            P(),
            P(),
            P(None, None, "tensor"),
            P(None, "tensor"),
            P("tensor", None),
            P(),
            P(),
            P(),
            P(None, "tensor"),
            P("tensor"),
            P("tensor", None),
            P(),
            P(("dp", "tensor"), None),
        ),
        out_specs=(
            P(("dp", "tensor"), None),
            P(("dp", "tensor"), None),
            P(None, "dp", "tensor"),
            P("tensor", "dp"),
            P("dp", "tensor"),
            P("tensor", "dp"),
            P(None, "tensor"),
            P("tensor"),
            P(),
            P("tensor"),
            P(None, None, "tensor"),
            P("tensor"),
        ),
        check_vma=False,
    )
```

profile of v0, /device:TPU:0, one launch (start us, length us, event | category | flops | bytes accessed | tf_op | source)
XLA Modules:
  0.0 802.8 jit_solution(1162977882640721757)
XLA Ops:
  12.5 26.6 %all-gather.5.cloned.1.call-done = bf16[1024,1152]{1,0:T(8,128)(2,1)} async-done(((bf16[256,1152]{1,0:T(8,128)(2,1)}), bf16[1024,1152]{1,0:T(8,128)(2,1)}) %all-gather.5.cloned.1.call-update) | async-done | bytes 2359312 | tf_op jit(solution)/shard_map/all_gather | solution.py:63
  39.2 4.7 fusion.54
  45.6 3.2 squeeze.52
  48.8 2.3 add_convert_fusion.2
  53.0 20.3 %while.51 = (s32[]{:T(128)}, bf16[2,512,4,72]{1,3,2,0:T(8,128)(2,1)}, f32[2,4,512]{2,1,0:T(4,128)S(1)}, f32[2,4]{1,0:T(2,128)S(1)}, s32[2,512]{1,0:T(2,128)S(1)}...) while((s32[]{:T(128)}, ...), condition=%wide.region_6.7_spmd, body=%wide.region_2.6_spmd.sunk | while | flops 631912448 | bytes 36186380 | solution.py:98
  53.4 2.8 fusion.132
  56.2 2.9 fusion.133
  59.2 3.1 fusion.134
  63.6 2.8 fusion.132
  66.4 2.9 fusion.133
  69.3 3.1 fusion.134
  76.0 3.6 fusion.82
  80.5 47.2 %reduce-scatter.11.cloned.1.call-done = f32[256,1152]{1,0:T(8,128)} async-done(((f32[1024,1152]{1,0:T(8,128)}), f32[256,1152]{1,0:T(8,128)}) %reduce-scatter.11.cloned.1.call-update) | async-done | bytes 1179664 | tf_op jit(solution)/shard_map/reduce_scatter | solution.py:104
  131.7 21.7 %all-gather.9.cloned.1.call-done = bf16[1024,1152]{1,0:T(8,128)(2,1)} async-done(((bf16[256,1152]{1,0:T(8,128)(2,1)}), bf16[1024,1152]{1,0:T(8,128)(2,1)}) %all-gather.9.cloned.1.call-update) | async-done | bytes 2359312 | tf_op jit(solution)/shard_map/all_gather | solution.py:128
  153.5 7.5 fusion.83
  161.0 18.6 %all-gather.7.cloned.1.call-done = bf16[1024,1152]{1,0:T(8,128)(2,1)} async-done(((bf16[256,1152]{1,0:T(8,128)(2,1)}), bf16[1024,1152]{1,0:T(8,128)(2,1)}) %all-gather.7.cloned.1.call-update) | async-done | bytes 2359312 | tf_op jit(solution)/shard_map/all_gather | solution.py:112
  179.6 9.9 %convert_reduce_fusion = (f32[1076]{0:T(1024)}, bf16[1024,1076]{0,1:T(8,128)(2,1)S(1)}, f32[1024,1076]{0,1:T(8,128)}) fusion(f32[1024,1076]{0,1:T(8,128)} %fusion.83, f32[1076]{0:T(1024)S(1)} %copy-done.48, bf16[1024,1152]{1,0:T(8,128)(2,1)} %all-gather.7.cloned.1.call-done, bf16[1152,1076]{0,1:T(8,128)(2,1)S(1)} %copy-done), kind=kOutput, calls=%fused_computation.63 | convolution fusion | flops 2563943424 | bytes 15865248 | tf_op jit(solution)/shard_map/dot_general | solution.py:113
  190.9 5.2 fusion.84
  197.8 7.5 convolution_convert_fusion
  205.4 38.8 %reduce-scatter.15.cloned.1.call-done = f32[256,1152]{1,0:T(8,128)} async-done(((f32[1024,1152]{1,0:T(8,128)}), f32[256,1152]{1,0:T(8,128)}) %reduce-scatter.15.cloned.1.call-update) | async-done | bytes 1179664 | tf_op jit(solution)/shard_map/reduce_scatter | solution.py:134
  244.1 2.4 multiply_reduce_fusion.1
  246.5 33.1 %reduce-scatter.13.cloned.1.call-done = bf16[256,1152]{1,0:T(8,128)(2,1)} async-done(((bf16[1024,1152]{1,0:T(8,128)(2,1)}), bf16[256,1152]{1,0:T(8,128)(2,1)}) %reduce-scatter.13.cloned.1.call-update) | async-done | bytes 589840 | tf_op jit(solution)/shard_map/reduce_scatter | solution.py:115
  279.6 3.6 fusion.77
  284.5 23.9 %all-gather.11.cloned.1.call-done = bf16[1024,1152]{1,0:T(8,128)(2,1)} async-done(((bf16[256,1152]{1,0:T(8,128)(2,1)}), bf16[1024,1152]{1,0:T(8,128)(2,1)}) %all-gather.11.cloned.1.call-update) | async-done | bytes 2359312 | tf_op jit(solution)/shard_map/all_gather | solution.py:143
  308.4 3.6 convolution_convert_fusion.1
  316.0 25.9 %while.52 = (s32[]{:T(128)}, f32[1024,4,72]{0,2,1:T(8,128)S(1)}, f32[1024,4,72]{0,2,1:T(8,128)}, bf16[2,512,4,72]{1,3,2,0:T(8,128)(2,1)}, bf16[2,512,4,72]{1,3,2...) while((s32[]{:T(128)}, f32[1024,4,72]{0,2,1:T(8,128)S(1)}, ...), condition=%wide.region_16.17_spmd.clone, body=%wide.region_14.16_spmd.clone.sunk | while | flops 1543698432 | bytes 91916632 | solution.py:188
  317.8 2.6 fusion.146
  320.5 3.3 multiply_reduce_fusion.7
  323.8 2.4 multiply_convert_fusion.6
  330.6 2.6 fusion.146
  333.3 3.3 multiply_reduce_fusion.7
  336.6 2.4 multiply_convert_fusion.6
  344.6 6.3 convolution_bitcast_fusion.1
  350.9 8.6 %copy.41 = f32[3,1152,288]{2,0,1:T(4,128)} copy(f32[3,1152,288]{1,2,0:T(8,128)} %convolution_bitcast_fusion.1) | data formatting | bytes 7962624
  359.5 9.0 %reshape.211 = f32[1152,864]{1,0:T(8,128)} reshape(f32[1152,3,288]{2,1,0:T(4,128)} %bitcast.143) | data formatting | bytes 7962624
  370.1 6.3 convolution_bitcast_fusion
  376.5 8.6 %fusion.76 = f32[1076,1152]{0,1:T(8,128)} fusion(bf16[1024,1152]{1,0:T(8,128)(2,1)} %all-gather.9.cloned.1.call-done, f32[1024,1076]{0,1:T(8,128)} %get-tuple-element.355), kind=kOutput, calls=%fused_computation.124 | convolution fusion | flops 2548518912 | bytes 11724800 | tf_op jit(solution)/shard_map/tf,td->fd/dot_general | solution.py:131
  385.4 8.0 fusion.86
  394.5 4.4 fusion.85
  399.1 22.0 %pmax.7 = f32[4]{0:T(128)S(1)} all-reduce(f32[4]{0:T(128)S(1)} %reduce_max.27), channel_id=1, replica_groups=mesh['dp'=8,'tensor'=4] {'dp'}, use_global_device_ids=true, to_apply=%region_37.38 | all-reduce | flops 4 | bytes 32 | tf_op jit(solution)/shard_map/pmax | solution.py:122
  423.7 34.2 %all-reduce = (f32[2,288]{1,0:T(2,128)}, f32[1076]{0:T(1024)}) all-reduce(f32[2,288]{1,0:T(2,128)S(1)} %pad_maximum_fusion.3, f32[1076]{0:T(1024)S(1)} %copy-done.43), channel_id=1, replica_groups=mesh['dp'=8,'tensor'=4] {'dp'}, use_global_device_ids=true, to_apply=%region_26.27 | all-reduce | flops 1652 | bytes 13216 | tf_op jit(solution)/shard_map/psum | solution.py:226
  457.9 2.4 reshape.212
  462.5 44.9 %reduce-scatter.17.cloned.1.call-done = f32[256,1152]{1,0:T(8,128)} async-done(((f32[1024,1152]{1,0:T(8,128)}), f32[256,1152]{1,0:T(8,128)}) %reduce-scatter.17.cloned.1.call-update) | async-done | bytes 1179664 | tf_op jit(solution)/shard_map/reduce_scatter | solution.py:211
  509.3 42.9 %psum.23 = f32[6,1152]{1,0:T(8,128)} all-reduce(f32[6,1152]{1,0:T(8,128)S(1)} %stack.43), channel_id=1, replica_groups=mesh['dp'=8,'tensor'=4] {'dp','tensor'}, use_global_device_ids=true, to_apply=%region_35.36 | all-reduce | flops 6912 | bytes 55296 | tf_op jit(solution)/shard_map/psum | solution.py:237
  552.2 2.9 fusion.69
  555.1 62.2 %reduce-scatter.23.cloned.1.call-done = f32[1076,144]{0,1:T(8,128)} async-done(((f32[1076,1152]{0,1:T(8,128)}), f32[1076,144]{0,1:T(8,128)}) %reduce-scatter.23.cloned.1.call-update) | async-done | bytes 619792 | tf_op jit(solution)/shard_map/reduce_scatter | solution.py:224
  617.3 108.1 %reduce-scatter.21.cloned.1.call-done = f32[144,1076]{1,0:T(8,128)} async-done(((f32[1152,1076]{1,0:T(8,128)}), f32[144,1076]{1,0:T(8,128)}) %reduce-scatter.21.cloned.1.call-update) | async-done | bytes 619792 | tf_op jit(solution)/shard_map/reduce_scatter | solution.py:223
  725.4 70.3 %reduce-scatter.19.cloned.1.call-done = f32[288,144]{0,1:T(8,128)} async-done(((f32[288,1152]{0,1:T(8,128)}), f32[288,144]{0,1:T(8,128)}) %reduce-scatter.19.cloned.1.call-update) | async-done | bytes 165904 | tf_op jit(solution)/shard_map/reduce_scatter | solution.py:222
  (219 shorter events, 47.9 us)
Async XLA Ops:
  7.2 172.5 %copy-start = (bf16[1152,1076]{0,1:T(8,128)(2,1)S(1)}, bf16[1152,1076]{0,1:T(8,128)(2,1)}, u32[]{:S(2)}) copy-start(bf16[1152,1076]{0,1:T(8,128)(2,1)} %param.29) | copy-start | bytes 7437316
  7.2 5.1 copy-start.27
  7.2 5.1 copy-start.44
  7.2 32.0 %all-gather.5.cloned.1.call-start = ((), (), s32[]{:S(2)}) async-start(), calls=%async_computation.8 | async-start | bytes 2949120 | tf_op jit(solution)/shard_map/all_gather | solution.py:63
  8.6 30.5 %copy-start.34 = (f32[256]{0:T(256)}, f32[256]{0:T(256)S(1)}, u32[]{:S(2)}) copy-start(f32[256]{0:T(256)S(1)} %broadcast_multiply_fusion.5) | copy-start | bytes 3076
  10.0 29.2 %copy-start.38 = (f32[256]{0:T(256)}, f32[256]{0:T(256)S(1)}, u32[]{:S(2)}) copy-start(f32[256]{0:T(256)S(1)} %add_rsqrt_fusion.1) | copy-start | bytes 3076
  12.2 115.5 %reduce-scatter.11.cloned.1.call-start = ((), (), s32[]{:S(2)}) async-start(), calls=%async_computation.9 | async-start | bytes 5898240 | tf_op jit(solution)/shard_map/reduce_scatter | solution.py:104
  12.4 31.6 %copy-start.36 = (f32[288]{0:T(512)}, f32[288]{0:T(512)S(1)}, u32[]{:S(2)}) copy-start(f32[288]{0:T(512)S(1)} %get-tuple-element.296) | copy-start | bytes 3460
  56.2 2.9 copy-start.16
  66.4 2.9 copy-start.16
  73.3 6.3 copy-start.45
  79.7 48.0 %copy-start.40 = (f32[1152]{0:T(1024)S(1)}, f32[1152]{0:T(1024)}, u32[]{:S(2)}) copy-start(f32[1152]{0:T(1024)} %param.26) | copy-start | bytes 13828
  79.7 50.7 %copy-start.28 = (f32[1152]{0:T(1024)S(1)}, f32[1152]{0:T(1024)}, u32[]{:S(2)}) copy-start(f32[1152]{0:T(1024)} %param.27) | copy-start | bytes 13828
  79.7 50.7 %copy-start.41 = (f32[1152]{0:T(1024)S(1)}, f32[1152]{0:T(1024)}, u32[]{:S(2)}) copy-start(f32[1152]{0:T(1024)} %param.28) | copy-start | bytes 13828
  79.7 73.7 %all-gather.9.cloned.1.call-start = ((), (), s32[]{:S(2)}) async-start(), calls=%async_computation.12 | async-start | bytes 2949120 | tf_op jit(solution)/shard_map/all_gather | solution.py:128
  80.5 99.2 %all-gather.7.cloned.1.call-start = ((), (), s32[]{:S(2)}) async-start(), calls=%async_computation.10 | async-start | bytes 2949120 | tf_op jit(solution)/shard_map/all_gather | solution.py:112
  131.5 48.1 %copy-start.48 = (f32[1076]{0:T(1024)S(1)}, f32[1076]{0:T(1024)}, u32[]{:S(2)}) copy-start(f32[1076]{0:T(1024)} %param.30) | copy-start | bytes 12916
  131.5 112.6 %reduce-scatter.15.cloned.1.call-start = ((), (), s32[]{:S(2)}) async-start(), calls=%async_computation.13 | async-start | bytes 5898240 | tf_op jit(solution)/shard_map/reduce_scatter | solution.py:134
  196.1 83.5 %reduce-scatter.13.cloned.1.call-start = ((), (), s32[]{:S(2)}) async-start(), calls=%async_computation.11 | async-start | bytes 2949120 | tf_op jit(solution)/shard_map/reduce_scatter | solution.py:115
  205.3 38.8 %copy-start.4 = (f32[256,1152]{1,0:T(8,128)S(1)}, f32[256,1152]{1,0:T(8,128)}, u32[]{:S(2)}) copy-start(f32[256,1152]{1,0:T(8,128)} %copy-done.3) | copy-start | bytes 3538948
  205.3 74.3 %copy-start.42 = (f32[1152]{0:T(1024)S(1)}, f32[1152]{0:T(1024)}, u32[]{:S(2)}) copy-start(f32[1152]{0:T(1024)} %param.32) | copy-start | bytes 13828
  205.3 103.1 %all-gather.11.cloned.1.call-start = ((), (), s32[]{:S(2)}) async-start(), calls=%async_computation.14 | async-start | bytes 2949120 | tf_op jit(solution)/shard_map/all_gather | solution.py:143
  283.2 25.2 %copy-start.8 = (f32[256,1152]{1,0:T(8,128)}, f32[256,1152]{1,0:T(8,128)S(1)}, u32[]{:S(2)}) copy-start(f32[256,1152]{1,0:T(8,128)S(1)} %get-tuple-element.340) | copy-start | bytes 3538948
  284.2 173.7 %reduce-scatter.25.cloned.1.call-start = ((), (), s32[]{:S(2)}) async-start(), calls=%async_computation.19 | async-start | bytes 4644864
  312.0 4.0 copy-start.2
  320.5 3.3 copy-start.19
  333.3 3.3 copy-start.19
  342.0 8.9 %copy-start.23 = (bf16[1024,4,72]{0,2,1:T(8,128)(2,1)}, bf16[1024,4,72]{0,2,1:T(8,128)(2,1)S(1)}, u32[]{:S(2)}) copy-start(bf16[1024,4,72]{0,2,1:T(8,128)(2,1)S(1)} %convert_element_type.109) | copy-start | bytes 1769476
  344.4 6.5 copy-start.25
  344.6 6.4 copy-start.26
  368.5 138.9 %reduce-scatter.17.cloned.1.call-start = ((), (), s32[]{:S(2)}) async-start(), calls=%async_computation.15 | async-start | bytes 5898240 | tf_op jit(solution)/shard_map/reduce_scatter | solution.py:211
  376.5 240.9 %reduce-scatter.23.cloned.1.call-start = ((), (), s32[]{:S(2)}) async-start(), calls=%async_computation.18 | async-start | bytes 5971968 | tf_op jit(solution)/shard_map/reduce_scatter | solution.py:224
  385.2 340.2 %reduce-scatter.21.cloned.1.call-start = ((), (), s32[]{:S(2)}) async-start(), calls=%async_computation.17 | async-start | bytes 5971968 | tf_op jit(solution)/shard_map/reduce_scatter | solution.py:223
  393.4 5.6 copy-start.46
  393.5 27.8 %copy-start.37 = (f32[288]{0:T(512)S(1)}, f32[288]{0:T(512)}, u32[]{:S(2)}) copy-start(f32[288]{0:T(512)} %copy-done.36) | copy-start | bytes 3460
  393.5 402.3 %reduce-scatter.19.cloned.1.call-start = ((), (), s32[]{:S(2)}) async-start(), calls=%async_computation.16 | async-start | bytes 1990656 | tf_op jit(solution)/shard_map/reduce_scatter | solution.py:222
  399.0 24.2 %copy-start.31 = (f32[1152]{0:T(1024)S(1)}, f32[1152]{0:T(1024)}, u32[]{:S(2)}) copy-start(f32[1152]{0:T(1024)} %get-tuple-element.287) | copy-start | bytes 13828
  399.0 24.2 %copy-start.33 = (f32[1152]{0:T(1024)S(1)}, f32[1152]{0:T(1024)}, u32[]{:S(2)}) copy-start(f32[1152]{0:T(1024)} %get-tuple-element.339) | copy-start | bytes 13828
  399.0 24.2 %copy-start.32 = (f32[1152]{0:T(1024)S(1)}, f32[1152]{0:T(1024)}, u32[]{:S(2)}) copy-start(f32[1152]{0:T(1024)} %get-tuple-element.354) | copy-start | bytes 13828
  399.0 24.3 %copy-start.30 = (f32[1152]{0:T(1024)S(1)}, f32[1152]{0:T(1024)}, u32[]{:S(2)}) copy-start(f32[1152]{0:T(1024)} %get-tuple-element.293) | copy-start | bytes 13828
  399.0 24.3 %copy-start.12 = (bf16[2,512,4,72]{1,3,2,0:T(8,128)(2,1)S(1)}, bf16[2,512,4,72]{1,3,2,0:T(8,128)(2,1)}, u32[]{:S(2)}) copy-start(bf16[2,512,4,72]{1,3,2,0:T(8,128)(2,1)} %get-tuple-element.176) | copy-start | bytes 1769476
  399.0 24.6 %copy-start.43 = (f32[1076]{0:T(1024)S(1)}, f32[1076]{0:T(1024)}, u32[]{:S(2)}) copy-start(f32[1076]{0:T(1024)} %get-tuple-element.341) | copy-start | bytes 12916
  421.1 39.2 %copy-start.49 = (f32[4]{0:T(128)}, f32[4]{0:T(128)S(1)}, u32[]{:S(2)}) copy-start(f32[4]{0:T(128)S(1)} %pmax.7) | copy-start | bytes 52
  423.2 84.2 %copy-start.7 = (bf16[256,1152]{1,0:T(8,128)(2,1)S(1)}, bf16[256,1152]{1,0:T(8,128)(2,1)}, u32[]{:S(2)}) copy-start(bf16[256,1152]{1,0:T(8,128)(2,1)} %param.19) | copy-start | bytes 1769476
  423.2 84.2 %copy-start.29 = (f32[1152]{0:T(1024)S(1)}, f32[1152]{0:T(1024)}, u32[]{:S(2)}) copy-start(f32[1152]{0:T(1024)} %param.21) | copy-start | bytes 13828
  423.2 84.2 %copy-start.35 = (f32[256]{0:T(256)S(1)}, f32[256]{0:T(256)}, u32[]{:S(2)}) copy-start(f32[256]{0:T(256)} %copy-done.34) | copy-start | bytes 3076
  423.2 84.2 %copy-start.39 = (f32[256]{0:T(256)S(1)}, f32[256]{0:T(256)}, u32[]{:S(2)}) copy-start(f32[256]{0:T(256)} %copy-done.38) | copy-start | bytes 3076
  460.3 335.5 %copy-start.1 = (bf16[1152,1076]{0,1:T(8,128)(2,1)S(1)}, bf16[1152,1076]{0,1:T(8,128)(2,1)}, u32[]{:S(2)}) copy-start(bf16[1152,1076]{0,1:T(8,128)(2,1)} %param.29) | copy-start | bytes 7437316
  (24 other events, 42.1 us)
Sparse Core Ops, SparseCore 0:
  12.4 26.7 all-gather.4
  79.8 47.8 reduce-scatter.10
  129.4 24.0 all-gather.8
  155.5 24.0 all-gather.6
  196.2 47.8 reduce-scatter.14
  246.5 33.0 reduce-scatter.12
  284.3 24.0 all-gather.10
  368.6 88.3 reduce-scatter.24
  459.6 47.7 reduce-scatter.16
  511.8 105.4 reduce-scatter.22
  621.5 103.8 reduce-scatter.20
  729.7 65.9 reduce-scatter.18
where the time goes:
time: 812 us; the launch traced here: 803 us
  waiting for transfers between devices  496 us (61%)
  matrix products  107 us (13%)
  blocking collectives  99.1 us (12%)
  local copies, waits for them, and re-layouts  46 us (6%)
  other arithmetic  37.6 us (5%)
  between operations  14.9 us (2%)
    reduce_scatter x1, waiting for transfers between devices, local(): lax.psum_scatter(grad_up, 'dp', scatter_dimension=0, tiled=True)  108 us
    reduce_scatter x1, waiting for transfers between devices, local(): lax.psum_scatter(grad_out, 'dp', scatter_dimension=1, tiled=True)  70.3 us
    reduce_scatter x1, waiting for transfers between devices, local(): lax.psum_scatter(grad_down, 'dp', scatter_dimension=1, tiled=True)  62.2 us
    reduce_scatter x1, waiting for transfers between devices, local(): lax.psum_scatter(jnp.dot(flat_att, w_out, preferred_element_type=jnp.floa...  47.2 us
    reduce_scatter x1, waiting for transfers between devices, local(): lax.psum_scatter(jnp.einsum('cte,cde->td', grad_stack, w_qkv, preferred_e...  44.9 us
    psum x1, blocking collectives, local(): grad_shared = lax.psum(shared_part, ('dp', 'tensor'))  42.9 us
    reduce_scatter x1, waiting for transfers between devices, local(): lax.psum_scatter(jnp.einsum('tf,df->td', grad_pre, w_up, preferred_elemen...  38.8 us
    psum x1, blocking collectives, local(): grad_qv_bias, grad_up_bias = lax.psum((grad_qv_bias, grad_up_bias), 'dp')  34.2 us
  transfers between devices with their start and end apart: 12, of which 11 were waited for; matrix products, arithmetic and copies ran while one was open for 7% of the time, Pallas kernels for 0%

commit v1 on v0

--- a/solution.py
+++ b/solution.py
@@ -109,7 +109,23 @@
     )
     residual = source + branch_a + out_bias
     normed_b, unit_b, inverse_b = normalize(residual, norm2_gain, norm2_bias)
-    whole_b = lax.all_gather(normed_b.astype(jnp.bfloat16), "tensor", axis=0, tiled=True)
+    shard = normed_b.astype(jnp.bfloat16)
+    size, index, rows = (lax.axis_size("tensor"), lax.axis_index("tensor"), shard.shape[0])
+    upward = [(i, (i + 1) % size) for i in range(size)]
+    left = [(i, (i - 1) % size) for i in range(size)]
+    out = jnp.zeros((*shard.shape[:0], size * rows, *shard.shape[0 + 1 :]), shard.dtype)
+    out = lax.dynamic_update_slice_in_dim(out, shard, index * rows, axis=0)
+    from_left = from_right = shard
+    half = size // 2
+    for turn in range(1, half + 1):
+        from_left = lax.ppermute(from_left, "tensor", upward)
+        out = lax.dynamic_update_slice_in_dim(out, from_left, (index - turn) % size * rows, axis=0)
+        if turn < size - half:
+            from_right = lax.ppermute(from_right, "tensor", left)
+            out = lax.dynamic_update_slice_in_dim(
+                out, from_right, (index + turn) % size * rows, axis=0
+            )
+    whole_b = out
     pre_act = jnp.dot(whole_b, w_up, preferred_element_type=jnp.float32) + up_bias
     activated = gelu_tanh(pre_act).astype(jnp.bfloat16)
     branch_b = lax.psum_scatter(

time: 812 us -> 804 us (level)
  waiting for transfers between devices: 496 us -> 485 us
    ppermute x0 -> x3, waiting for transfers between devices: none -> 22.4 us  [the longest x2 22.4 us: local(): from_left = lax.ppermute(from_left, 'tensor', upward)]
    all_gather x1 -> x0, waiting for transfers between devices: 18.6 us -> none  [local(): lax.all_gather(normed_b.astype(jnp.bfloat16), 'tensor', axis=0, tiled=True)]
    all_gather x1, waiting for transfers between devices: 21.7 us -> 6.45 us  [local(): whole_grad = lax.all_gather(cotangent, 'tensor', axis=0, tiled=True)]
    unnamed x90 -> x98, local copies, waits for them, and re-layouts: 30.4 us -> 34.3 us
  transfers between devices with their start and end apart: 12 -> 14, of which waited for: 11 -> 11; matrix products, arithmetic and copies ran while one was open for 7% -> 7% of each run, Pallas kernels for 0% -> 0%
where the time goes in v1:
time: 804 us; the launch traced here: 794 us
  waiting for transfers between devices  485 us (60%)
  matrix products  102 us (13%)
  blocking collectives  98.5 us (12%)
  local copies, waits for them, and re-layouts  53.3 us (7%)
  other arithmetic  37.6 us (5%)
  between operations  14.7 us (2%)
    reduce_scatter x1, waiting for transfers between devices, local(): lax.psum_scatter(grad_up, 'dp', scatter_dimension=0, tiled=True)  108 us
    reduce_scatter x1, waiting for transfers between devices, local(): lax.psum_scatter(grad_out, 'dp', scatter_dimension=1, tiled=True)  70.8 us
    reduce_scatter x1, waiting for transfers between devices, local(): lax.psum_scatter(grad_down, 'dp', scatter_dimension=1, tiled=True)  62.1 us
    reduce_scatter x1, waiting for transfers between devices, local(): lax.psum_scatter(jnp.dot(flat_att, w_out, preferred_element_type=jnp.floa...  47.2 us
    reduce_scatter x1, waiting for transfers between devices, local(): lax.psum_scatter(jnp.einsum('cte,cde->td', grad_stack, w_qkv, preferred_e...  43.8 us
    psum x1, blocking collectives, local(): grad_shared = lax.psum(shared_part, ('dp', 'tensor'))  42.9 us
    reduce_scatter x1, waiting for transfers between devices, local(): lax.psum_scatter(jnp.einsum('tf,df->td', grad_pre, w_up, preferred_elemen...  39.7 us
    unnamed x98, local copies, waits for them, and re-layouts  34.3 us
  transfers between devices with their start and end apart: 14, of which 11 were waited for; matrix products, arithmetic and copies ran while one was open for 7% of the time, Pallas kernels for 0%

profile of v1, /device:TPU:0, one launch (start us, length us, event | category | flops | bytes accessed | tf_op | source)
XLA Modules:
  0.0 794.4 jit_solution(15693201338768473282)
XLA Ops:
  12.5 26.6 %all-gather.4.cloned.1.call-done = bf16[1024,1152]{1,0:T(8,128)(2,1)} async-done(((bf16[256,1152]{1,0:T(8,128)(2,1)}), bf16[1024,1152]{1,0:T(8,128)(2,1)}) %all-gather.4.cloned.1.call-update) | async-done | bytes 2359312 | tf_op jit(solution)/shard_map/all_gather | solution.py:63
  39.2 4.7 fusion.54
  45.6 3.2 squeeze.52
  48.8 2.3 add_convert_fusion.2
  53.0 20.3 %while.51 = (s32[]{:T(128)}, bf16[2,512,4,72]{1,3,2,0:T(8,128)(2,1)}, f32[2,4,512]{2,1,0:T(4,128)S(1)}, f32[2,4]{1,0:T(2,128)S(1)}, s32[2,512]{1,0:T(2,128)S(1)}...) while((s32[]{:T(128)}, ...), condition=%wide.region_6.7_spmd, body=%wide.region_2.6_spmd.sunk | while | flops 631912448 | bytes 36186380 | solution.py:98
  53.4 2.8 fusion.132
  56.2 2.9 fusion.133
  59.2 3.1 fusion.134
  63.6 2.8 fusion.132
  66.4 2.9 fusion.133
  69.4 3.1 fusion.134
  76.1 3.6 fusion.82
  80.5 47.2 %reduce-scatter.11.cloned.1.call-done = f32[256,1152]{1,0:T(8,128)} async-done(((f32[1024,1152]{1,0:T(8,128)}), f32[256,1152]{1,0:T(8,128)}) %reduce-scatter.11.cloned.1.call-update) | async-done | bytes 1179664 | tf_op jit(solution)/shard_map/reduce_scatter | solution.py:104
  134.7 22.4 %collective-permute-done = bf16[256,1152]{1,0:T(8,128)(2,1)} collective-permute-done((bf16[256,1152]{1,0:T(8,128)(2,1)}, bf16[256,1152]{1,0:T(8,128)(2,1)}, u32[]{:S(2)}, u32[]{:S(2)}) %collective-permute-start) | collective-permute-done | bytes 589856 | tf_op jit(solution)/shard_map/ppermute | solution.py:121
  157.1 6.5 all-gather.6.cloned.1.call-done
  163.5 5.6 fusion.83
  172.7 7.8 convert_reduce_fusion
  181.9 5.2 fusion.84
  188.8 7.4 convolution_convert_fusion
  196.3 39.7 %reduce-scatter.15.cloned.1.call-done = f32[256,1152]{1,0:T(8,128)} async-done(((f32[1024,1152]{1,0:T(8,128)}), f32[256,1152]{1,0:T(8,128)}) %reduce-scatter.15.cloned.1.call-update) | async-done | bytes 1179664 | tf_op jit(solution)/shard_map/reduce_scatter | solution.py:150
  236.0 2.4 multiply_reduce_fusion.1
  238.4 33.1 %reduce-scatter.13.cloned.1.call-done = bf16[256,1152]{1,0:T(8,128)(2,1)} async-done(((bf16[1024,1152]{1,0:T(8,128)(2,1)}), bf16[256,1152]{1,0:T(8,128)(2,1)}) %reduce-scatter.13.cloned.1.call-update) | async-done | bytes 589840 | tf_op jit(solution)/shard_map/reduce_scatter | solution.py:131
  271.5 3.6 fusion.77
  276.4 23.9 %all-gather.8.cloned.1.call-done = bf16[1024,1152]{1,0:T(8,128)(2,1)} async-done(((bf16[256,1152]{1,0:T(8,128)(2,1)}), bf16[1024,1152]{1,0:T(8,128)(2,1)}) %all-gather.8.cloned.1.call-update) | async-done | bytes 2359312 | tf_op jit(solution)/shard_map/all_gather | solution.py:159
  300.3 3.6 convolution_convert_fusion.1
  307.9 25.9 %while.52 = (s32[]{:T(128)}, f32[1024,4,72]{0,2,1:T(8,128)S(1)}, f32[1024,4,72]{0,2,1:T(8,128)}, bf16[2,512,4,72]{1,3,2,0:T(8,128)(2,1)}, bf16[2,512,4,72]{1,3,2...) while((s32[]{:T(128)}, f32[1024,4,72]{0,2,1:T(8,128)S(1)}, ...), condition=%wide.region_16.17_spmd.clone, body=%wide.region_14.16_spmd.clone.sunk | while | flops 1543698432 | bytes 91916632 | solution.py:204
  309.8 2.6 fusion.146
  312.4 3.3 multiply_reduce_fusion.7
  315.7 2.4 multiply_convert_fusion.6
  322.5 2.6 fusion.146
  325.2 3.3 multiply_reduce_fusion.7
  328.5 2.4 multiply_convert_fusion.6
  336.3 6.4 convolution_bitcast_fusion.1
  342.6 8.6 %copy.41 = f32[3,1152,288]{2,0,1:T(4,128)} copy(f32[3,1152,288]{1,2,0:T(8,128)} %convolution_bitcast_fusion.1) | data formatting | bytes 7962624
  351.2 8.9 %reshape.211 = f32[1152,864]{1,0:T(8,128)} reshape(f32[1152,3,288]{2,1,0:T(4,128)} %bitcast.143) | data formatting | bytes 7962624
  361.7 6.3 convolution_bitcast_fusion
  369.7 7.9 fusion.76
  379.3 7.3 fusion.86
  387.7 4.6 fusion.85
  392.4 21.8 %pmax.7 = f32[4]{0:T(128)S(1)} all-reduce(f32[4]{0:T(128)S(1)} %reduce_max.27), channel_id=1, replica_groups=mesh['dp'=8,'tensor'=4] {'dp'}, use_global_device_ids=true, to_apply=%region_37.38 | all-reduce | flops 4 | bytes 32 | tf_op jit(solution)/shard_map/pmax | solution.py:138
  416.8 33.8 %all-reduce = (f32[2,288]{1,0:T(2,128)}, f32[1076]{0:T(1024)}) all-reduce(f32[2,288]{1,0:T(2,128)S(1)} %pad_maximum_fusion.3, f32[1076]{0:T(1024)S(1)} %copy-done.46), channel_id=1, replica_groups=mesh['dp'=8,'tensor'=4] {'dp'}, use_global_device_ids=true, to_apply=%region_26.27 | all-reduce | flops 1652 | bytes 13216 | tf_op jit(solution)/shard_map/psum | solution.py:242
  450.5 2.4 reshape.212
  455.1 43.8 %reduce-scatter.17.cloned.1.call-done = f32[256,1152]{1,0:T(8,128)} async-done(((f32[1024,1152]{1,0:T(8,128)}), f32[256,1152]{1,0:T(8,128)}) %reduce-scatter.17.cloned.1.call-update) | async-done | bytes 1179664 | tf_op jit(solution)/shard_map/reduce_scatter | solution.py:227
  500.9 42.9 %psum.23 = f32[6,1152]{1,0:T(8,128)} all-reduce(f32[6,1152]{1,0:T(8,128)S(1)} %stack.43), channel_id=1, replica_groups=mesh['dp'=8,'tensor'=4] {'dp','tensor'}, use_global_device_ids=true, to_apply=%region_35.36 | all-reduce | flops 6912 | bytes 55296 | tf_op jit(solution)/shard_map/psum | solution.py:253
  543.9 2.9 fusion.69
  546.8 62.1 %reduce-scatter.23.cloned.1.call-done = f32[1076,144]{0,1:T(8,128)} async-done(((f32[1076,1152]{0,1:T(8,128)}), f32[1076,144]{0,1:T(8,128)}) %reduce-scatter.23.cloned.1.call-update) | async-done | bytes 619792 | tf_op jit(solution)/shard_map/reduce_scatter | solution.py:240
  608.8 108.0 %reduce-scatter.21.cloned.1.call-done = f32[144,1076]{1,0:T(8,128)} async-done(((f32[1152,1076]{1,0:T(8,128)}), f32[144,1076]{1,0:T(8,128)}) %reduce-scatter.21.cloned.1.call-update) | async-done | bytes 619792 | tf_op jit(solution)/shard_map/reduce_scatter | solution.py:239
  716.9 70.8 %reduce-scatter.19.cloned.1.call-done = f32[288,144]{0,1:T(8,128)} async-done(((f32[288,1152]{0,1:T(8,128)}), f32[288,144]{0,1:T(8,128)}) %reduce-scatter.19.cloned.1.call-update) | async-done | bytes 165904 | tf_op jit(solution)/shard_map/reduce_scatter | solution.py:238
  (234 shorter events, 56.9 us)
Async XLA Ops:
  7.2 165.5 %copy-start = (bf16[1152,1076]{0,1:T(8,128)(2,1)S(1)}, bf16[1152,1076]{0,1:T(8,128)(2,1)}, u32[]{:S(2)}) copy-start(bf16[1152,1076]{0,1:T(8,128)(2,1)} %param.29) | copy-start | bytes 7437316
  7.2 5.1 copy-start.30
  7.2 5.1 copy-start.47
  7.2 32.0 %all-gather.4.cloned.1.call-start = ((), (), s32[]{:S(2)}) async-start(), calls=%async_computation.8 | async-start | bytes 2949120 | tf_op jit(solution)/shard_map/all_gather | solution.py:63
  8.6 30.5 %copy-start.37 = (f32[256]{0:T(256)}, f32[256]{0:T(256)S(1)}, u32[]{:S(2)}) copy-start(f32[256]{0:T(256)S(1)} %broadcast_multiply_fusion.5) | copy-start | bytes 3076
  10.0 29.2 %copy-start.41 = (f32[256]{0:T(256)}, f32[256]{0:T(256)S(1)}, u32[]{:S(2)}) copy-start(f32[256]{0:T(256)S(1)} %add_rsqrt_fusion.1) | copy-start | bytes 3076
  12.2 115.5 %reduce-scatter.11.cloned.1.call-start = ((), (), s32[]{:S(2)}) async-start(), calls=%async_computation.9 | async-start | bytes 5898240 | tf_op jit(solution)/shard_map/reduce_scatter | solution.py:104
  12.4 31.6 %copy-start.39 = (f32[288]{0:T(512)}, f32[288]{0:T(512)S(1)}, u32[]{:S(2)}) copy-start(f32[288]{0:T(512)S(1)} %get-tuple-element.296) | copy-start | bytes 3460
  73.4 6.3 copy-start.48
  79.7 48.0 %copy-start.43 = (f32[1152]{0:T(1024)S(1)}, f32[1152]{0:T(1024)}, u32[]{:S(2)}) copy-start(f32[1152]{0:T(1024)} %param.26) | copy-start | bytes 13828
  79.7 83.8 %all-gather.6.cloned.1.call-start = ((), (), s32[]{:S(2)}) async-start(), calls=%async_computation.11 | async-start | bytes 2949120 | tf_op jit(solution)/shard_map/all_gather | solution.py:144
  80.5 155.6 %reduce-scatter.15.cloned.1.call-start = ((), (), s32[]{:S(2)}) async-start(), calls=%async_computation.12 | async-start | bytes 5898240 | tf_op jit(solution)/shard_map/reduce_scatter | solution.py:150
  132.8 24.3 %collective-permute-start = (bf16[256,1152]{1,0:T(8,128)(2,1)}, bf16[256,1152]{1,0:T(8,128)(2,1)}, u32[]{:S(2)}, u32[]{:S(2)}) collective-permute-start(bf16[256,1152]{1,0:T(8,128)(2,1)} %get-tuple-element.346), channel_id=1, source_target_pairs={{0,1},{1,2},{2,3},{3,0},{4,5},{5,6},{6,7},{7,4},{8,9},{9,10},{10,1... | collective-permute-start | bytes 1769480 | tf_op jit(solution)/shard_map/ppermute | solution.py:121
  133.0 37.3 %collective-permute-start.1 = (bf16[256,1152]{1,0:T(8,128)(2,1)}, bf16[256,1152]{1,0:T(8,128)(2,1)}, u32[]{:S(2)}, u32[]{:S(2)}) collective-permute-start(bf16[256,1152]{1,0:T(8,128)(2,1)} %get-tuple-element.346), channel_id=1, source_target_pairs={{0,3},{1,0},{2,1},{3,2},{4,7},{5,4},{6,5},{7,6},{8,11},{9,8},{10,9... | collective-permute-start | bytes 1769480 | tf_op jit(solution)/shard_map/ppermute | solution.py:124
  157.1 14.4 %collective-permute-start.2 = (bf16[256,1152]{1,0:T(8,128)(2,1)}, bf16[256,1152]{1,0:T(8,128)(2,1)}, u32[]{:S(2)}, u32[]{:S(2)}) collective-permute-start(bf16[256,1152]{1,0:T(8,128)(2,1)} %collective-permute-done), channel_id=1, source_target_pairs={{0,1},{1,2},{2,3},{3,0},{4,5},{5,6},{6,7},{7,4},{8,9},{9,10},{10,1... | collective-permute-start | bytes 1769480 | tf_op jit(solution)/shard_map/ppermute | solution.py:121
  163.5 5.7 copy-start.17
  169.2 3.5 copy-start.52
  172.7 7.8 copy-start.18
  187.1 84.4 %reduce-scatter.13.cloned.1.call-start = ((), (), s32[]{:S(2)}) async-start(), calls=%async_computation.10 | async-start | bytes 2949120 | tf_op jit(solution)/shard_map/reduce_scatter | solution.py:131
  196.2 39.8 %copy-start.4 = (f32[256,1152]{1,0:T(8,128)S(1)}, f32[256,1152]{1,0:T(8,128)}, u32[]{:S(2)}) copy-start(f32[256,1152]{1,0:T(8,128)} %copy-done.3) | copy-start | bytes 3538948
  196.2 75.3 %copy-start.45 = (f32[1152]{0:T(1024)S(1)}, f32[1152]{0:T(1024)}, u32[]{:S(2)}) copy-start(f32[1152]{0:T(1024)} %param.32) | copy-start | bytes 13828
  196.2 104.1 %all-gather.8.cloned.1.call-start = ((), (), s32[]{:S(2)}) async-start(), calls=%async_computation.13 | async-start | bytes 2949120 | tf_op jit(solution)/shard_map/all_gather | solution.py:159
  275.1 25.2 %copy-start.8 = (f32[256,1152]{1,0:T(8,128)}, f32[256,1152]{1,0:T(8,128)S(1)}, u32[]{:S(2)}) copy-start(f32[256,1152]{1,0:T(8,128)S(1)} %get-tuple-element.340) | copy-start | bytes 3538948
  276.1 174.4 %reduce-scatter.25.cloned.1.call-start = ((), (), s32[]{:S(2)}) async-start(), calls=%async_computation.18 | async-start | bytes 4644864
  303.9 4.0 copy-start.2
  312.4 3.3 copy-start.23
  325.2 3.3 copy-start.23
  336.1 6.6 copy-start.28
  336.3 6.4 copy-start.29
  360.2 138.8 %reduce-scatter.17.cloned.1.call-start = ((), (), s32[]{:S(2)}) async-start(), calls=%async_computation.14 | async-start | bytes 5898240 | tf_op jit(solution)/shard_map/reduce_scatter | solution.py:227
  368.1 240.8 %reduce-scatter.23.cloned.1.call-start = ((), (), s32[]{:S(2)}) async-start(), calls=%async_computation.17 | async-start | bytes 5971968 | tf_op jit(solution)/shard_map/reduce_scatter | solution.py:240
  377.6 339.3 %reduce-scatter.21.cloned.1.call-start = ((), (), s32[]{:S(2)}) async-start(), calls=%async_computation.16 | async-start | bytes 5971968 | tf_op jit(solution)/shard_map/reduce_scatter | solution.py:239
  386.6 5.7 copy-start.49
  386.6 27.7 %copy-start.40 = (f32[288]{0:T(512)S(1)}, f32[288]{0:T(512)}, u32[]{:S(2)}) copy-start(f32[288]{0:T(512)} %copy-done.39) | copy-start | bytes 3460
  386.6 401.0 %reduce-scatter.19.cloned.1.call-start = ((), (), s32[]{:S(2)}) async-start(), calls=%async_computation.15 | async-start | bytes 1990656 | tf_op jit(solution)/shard_map/reduce_scatter | solution.py:238
  387.7 27.2 %copy-start.26 = (bf16[3,1152,288]{1,2,0:T(8,128)(2,1)S(1)}, bf16[3,1152,288]{1,2,0:T(8,128)(2,1)}, u32[]{:S(2)}) copy-start(bf16[3,1152,288]{1,2,0:T(8,128)(2,1)} %param.23) | copy-start | bytes 5971972
  392.3 24.0 %copy-start.34 = (f32[1152]{0:T(1024)S(1)}, f32[1152]{0:T(1024)}, u32[]{:S(2)}) copy-start(f32[1152]{0:T(1024)} %get-tuple-element.287) | copy-start | bytes 13828
  392.3 24.0 %copy-start.36 = (f32[1152]{0:T(1024)S(1)}, f32[1152]{0:T(1024)}, u32[]{:S(2)}) copy-start(f32[1152]{0:T(1024)} %get-tuple-element.339) | copy-start | bytes 13828
  392.3 24.1 %copy-start.35 = (f32[1152]{0:T(1024)S(1)}, f32[1152]{0:T(1024)}, u32[]{:S(2)}) copy-start(f32[1152]{0:T(1024)} %get-tuple-element.356) | copy-start | bytes 13828
  392.3 24.1 %copy-start.33 = (f32[1152]{0:T(1024)S(1)}, f32[1152]{0:T(1024)}, u32[]{:S(2)}) copy-start(f32[1152]{0:T(1024)} %get-tuple-element.293) | copy-start | bytes 13828
  392.3 24.1 %copy-start.12 = (bf16[2,512,4,72]{1,3,2,0:T(8,128)(2,1)S(1)}, bf16[2,512,4,72]{1,3,2,0:T(8,128)(2,1)}, u32[]{:S(2)}) copy-start(bf16[2,512,4,72]{1,3,2,0:T(8,128)(2,1)} %get-tuple-element.176) | copy-start | bytes 1769476
  392.3 24.5 %copy-start.46 = (f32[1076]{0:T(1024)S(1)}, f32[1076]{0:T(1024)}, u32[]{:S(2)}) copy-start(f32[1076]{0:T(1024)} %get-tuple-element.341) | copy-start | bytes 12916
  414.2 38.8 %copy-start.53 = (f32[4]{0:T(128)}, f32[4]{0:T(128)S(1)}, u32[]{:S(2)}) copy-start(f32[4]{0:T(128)S(1)} %pmax.7) | copy-start | bytes 52
  416.3 82.7 %copy-start.7 = (bf16[256,1152]{1,0:T(8,128)(2,1)S(1)}, bf16[256,1152]{1,0:T(8,128)(2,1)}, u32[]{:S(2)}) copy-start(bf16[256,1152]{1,0:T(8,128)(2,1)} %param.19) | copy-start | bytes 1769476
  416.3 82.7 %copy-start.32 = (f32[1152]{0:T(1024)S(1)}, f32[1152]{0:T(1024)}, u32[]{:S(2)}) copy-start(f32[1152]{0:T(1024)} %param.21) | copy-start | bytes 13828
  416.3 82.7 %copy-start.38 = (f32[256]{0:T(256)S(1)}, f32[256]{0:T(256)}, u32[]{:S(2)}) copy-start(f32[256]{0:T(256)} %copy-done.37) | copy-start | bytes 3076
  416.3 82.7 %copy-start.42 = (f32[256]{0:T(256)S(1)}, f32[256]{0:T(256)}, u32[]{:S(2)}) copy-start(f32[256]{0:T(256)} %copy-done.41) | copy-start | bytes 3076
  452.9 334.7 %copy-start.1 = (bf16[1152,1076]{0,1:T(8,128)(2,1)S(1)}, bf16[1152,1076]{0,1:T(8,128)(2,1)}, u32[]{:S(2)}) copy-start(bf16[1152,1076]{0,1:T(8,128)(2,1)} %param.29) | copy-start | bytes 7437316
  (30 other events, 53.3 us)
Sparse Core Ops, SparseCore 0:
  12.4 26.7 all-gather.3
  79.8 47.8 reduce-scatter.10
  129.4 34.1 all-gather.5
  187.2 48.7 reduce-scatter.14
  238.4 33.0 reduce-scatter.12
  276.2 24.0 all-gather.7
  360.3 88.3 reduce-scatter.24
  451.2 47.6 reduce-scatter.16
  503.6 105.2 reduce-scatter.22
  612.9 103.9 reduce-scatter.20
  721.3 66.2 reduce-scatter.18
